TPU v7x, 128 devices: a whole 4x4x4 slice. The times are simulated.
128 devices in a mesh: rep: 8 (over z, y_hi), slab: 16 (over y_lo, x, core).
Axes of the slice: x: 4, y: 4 (y_hi: 2, y_lo: 2; y = y_hi * 2 + y_lo), z: 4, core: 2. Of those that a mesh axis runs over, the one named last changes fastest.
Arguments:
- feats: bfloat16 [8, 32, 24576], P('rep', None, 'slab'), may hold values from -6 to 6
- tile_weight: bfloat16 [8, 1536, 64, 512], P('rep', 'slab'), may hold values from -0.25 to 0.25
- tile_atom: int32 [8, 1536], P('rep', 'slab'), may hold values from 0 to 23
- tile_cell: int32 [8, 1536], P('rep', 'slab'), may hold values from 0 to 31
- tile_live: int32 [8, 16], P('rep', 'slab'), may hold values from 24 to 96, as said below
- w_mix: bfloat16 [32, 32], replicated, may hold values from -1 to 1
- conv_w: bfloat16 [27, 32, 32], replicated, may hold values from -0.21875 to 0.21875
- cotangent: bfloat16 [8, 32, 24576], P('rep', None, 'slab'), may hold values from -6 to 6
Outputs:
- potential: bfloat16 [8, 32, 24576], P('rep', None, 'slab')
- grad_feats: bfloat16 [8, 32, 24576], P('rep', None, 'slab')
- grad_conv: float32 [27, 32, 32], replicated
- grad_mix: float32 [32, 32], replicated
Inputs may be any that keep to these rules, and one draw needn't show every extreme that they name: The first tile_live slots of a slab's list are live, the rest are ignored; in every system some slab has all 96 slots live. `tile_atom`: atom block within the tile's own slab. `tile_cell`: cell block within the slab's window of 8 planes that starts 2 planes below the slab.
All inputs are finite; a program needn't handle non-finite values.
Results may differ from a plain program's by a relative error of at most 0.013.
Values may be sent and summed in bfloat16 or wider, within the bound.
A program may use at most 128 MiB of HBM per device.

v0:
```python
import math
import jax
import jax.numpy as jnp
from jax import lax
from jax.sharding import PartitionSpec as P

C = 32
GY = 32
GX = 64
ZD = 4
ZH = 2
A_DEV = 1536
TILE_A = 64
TILE_C = 512
PW = 8
NB = 32
NAB = 24


def from_behind(value, axis, steps):
    count = lax.axis_size(axis)
    pairs = [(source, (source + steps) % count) for source in range(count)]
    return lax.ppermute(value, axis, pairs)


def extended_2(block, sides, width):
    for axis, dim in sides:
        count = lax.axis_size(axis)
        forward = [(i, i + 1) for i in range(count - 1)]
        forward.append((count - 1, 0))
        backward = [(target, source) for source, target in forward]
        low = lax.ppermute(
            lax.slice_in_dim(block, block.shape[dim] - width, None, axis=dim), axis, forward
        )
        high = lax.ppermute(lax.slice_in_dim(block, 0, width, axis=dim), axis, backward)
        block = jnp.concatenate([low, block, high], axis=dim)
    return block


def shifted_stack(field):
    planes = field.shape[1]
    shaped = field.reshape(C, planes, GY, GX)
    pieces = []
    for row_off in (-1, 0, 1):
        for col_off in (-1, 0, 1):
            rolled = jnp.roll(shaped, (-row_off, -col_off), (2, 3))
            pieces.append(rolled.reshape(C, planes, GY * GX))
    return jnp.concatenate(pieces, axis=0)


def conv_valid(field, kernel_set):
    planes = field.shape[1] - 2
    stacked = shifted_stack(field)
    result = jnp.zeros((C, planes, GY * GX), jnp.float32)
    for plane_off in range(3):
        kernel = jnp.transpose(kernel_set[plane_off * 9 : (plane_off + 1) * 9], (1, 0, 2)).reshape(
            C, 9 * C
        )
        result = result + jnp.einsum(
            "ok,kpn->opn",
            kernel,
            stacked[:, plane_off : plane_off + planes],
            preferred_element_type=jnp.float32,
        )
    return result


def weight_grad(upstream, field):
    planes = upstream.shape[1]
    stacked = shifted_stack(field)
    collected = []
    for plane_off in range(3):
        product = jnp.einsum(
            "opn,kpn->ok",
            upstream,
            stacked[:, plane_off : plane_off + planes],
            preferred_element_type=jnp.float32,
        )
        collected.append(jnp.transpose(product.reshape(C, 9, C), (1, 0, 2)))
    return jnp.concatenate(collected, axis=0)


def deposit_tiles(source, weights, atom_ids, first_tile, live_tiles):
    blocks = source.reshape(C, NAB, TILE_A)
    picked = jnp.take(blocks, atom_ids, axis=1)
    product = jnp.einsum("ctk,tkn->tcn", picked, weights, preferred_element_type=jnp.float32)
    alive = first_tile + jnp.arange(weights.shape[0], dtype=jnp.int32) < live_tiles
    return jnp.where(alive[:, None, None], product, 0.0)


def collect_tiles(window_blocks, weights, cell_ids, first_tile, live_tiles):
    picked = jnp.take(window_blocks, cell_ids, axis=1)
    product = jnp.einsum("ctn,tkn->tck", picked, weights, preferred_element_type=jnp.float32)
    alive = first_tile + jnp.arange(weights.shape[0], dtype=jnp.int32) < live_tiles
    return jnp.where(alive[:, None, None], product, 0.0)


def over_tiles(tile_fn, operand, weights, source_ids, target_ids, live_tiles, segments):
    products = tile_fn(operand, weights, source_ids, 0, live_tiles)
    return jax.ops.segment_sum(products, target_ids, num_segments=segments)


def fold_rims(window):
    upper_rim = window[:, ZH + ZD :]
    lower_rim = window[:, :ZH]
    from_below = from_behind(upper_rim.astype(jnp.bfloat16), "slab", 1).astype(upper_rim.dtype)
    from_above = from_behind(lower_rim.astype(jnp.bfloat16), "slab", -1).astype(lower_rim.dtype)
    owned = window[:, ZH : ZH + ZD]
    owned = owned.at[:, :ZH].add(from_below)
    owned = owned.at[:, ZD - ZH :].add(from_above)
    return owned


def with_near(field):
    return extended_2(field, (("slab", 1),), 1)


def with_read(field):
    return extended_2(field, (("slab", 1),), ZH)


def local(feats, tile_weight, tile_atom, tile_cell, tile_live, w_mix, conv_w, cotangent):
    atom_feats = feats[0]
    weights = tile_weight[0]
    atom_ids = tile_atom[0]
    cell_ids = tile_cell[0]
    live_tiles = tile_live[0, 0]
    kernel_flip = jnp.transpose(conv_w[::-1], (0, 2, 1))

    def spread_mesh(source):
        sums = over_tiles(deposit_tiles, source, weights, atom_ids, cell_ids, live_tiles, NB)
        window = jnp.transpose(sums, (1, 0, 2)).reshape(C, PW, GY * GX)
        return fold_rims(window)

    def gather_atoms(extended):
        window_blocks = extended.reshape(C, NB, TILE_C)
        sums = over_tiles(
            collect_tiles, window_blocks, weights, cell_ids, atom_ids, live_tiles, NAB
        )
        return jnp.transpose(sums, (1, 0, 2)).reshape(C, A_DEV)

    mixed = jnp.dot(w_mix, atom_feats, preferred_element_type=jnp.float32).astype(jnp.bfloat16)
    density = spread_mesh(mixed).astype(jnp.bfloat16)
    density_near = with_near(density)
    field_mesh = with_read(conv_valid(density_near, conv_w).astype(jnp.bfloat16))
    potential = gather_atoms(field_mesh).astype(jnp.bfloat16)
    mesh_grad = spread_mesh(cotangent[0]).astype(jnp.bfloat16)
    density_grad = with_read(conv_valid(with_near(mesh_grad), kernel_flip).astype(jnp.bfloat16))
    mixed_grad = gather_atoms(density_grad).astype(jnp.bfloat16)
    feats_grad = jnp.dot(w_mix.T, mixed_grad, preferred_element_type=jnp.float32).astype(
        jnp.bfloat16
    )
    conv_part = weight_grad(mesh_grad, density_near)
    mix_part = lax.dot_general(
        mixed_grad, atom_feats, (((1,), (1,)), ((), ())), preferred_element_type=jnp.float32
    )
    conv_total, mix_total = lax.psum((conv_part, mix_part), ("rep", "slab"))
    groups = lax.axis_size("rep") * lax.axis_size("slab")
    conv_scale = math.sqrt(groups * ZD * GY * GX)
    mix_scale = math.sqrt(groups * A_DEV)
    return (potential[None], feats_grad[None], conv_total / conv_scale, mix_total / mix_scale)


def solution(mesh):
    return jax.shard_map(
        local,
        mesh=mesh,
        in_specs=(
            P("rep", None, "slab"),
            P("rep", "slab", None, None),
            P("rep", "slab"),
            P("rep", "slab"),
            P("rep", "slab"),
            P(),
            P(),
            P("rep", None, "slab"),
        ),
        out_specs=(P("rep", None, "slab"), P("rep", None, "slab"), P(), P()),
        check_vma=False,
    )
```

profile of v0, /device:TPU:1, one launch (start us, length us, event | category | flops | bytes accessed | tf_op | source)
XLA Modules:
  0.0 452.7 jit_solution(4543794386522970593)
XLA Ops:
  11.0 6.5 %broadcast_select_fusion.1 = f32[96,32,512]{2,1,0:T(8,128)} fusion(pred[96]{0:T(512)(128)(4,1)S(1)} %iota_compare_fusion, bf16[1,96,64,512]{3,2,1,0:T(8,128)(2,1)} %param.21, bf16[96,32,64]{2,1,0:T(8,128)(2,1)S(1)} %gather_fusion, pred[96]{0:T(512)(128)(4,1)S(1)} %get-tuple-element.115), kind=kOutput, calls=%fused_computation.47 | convolution fusion | flops 203096064 | bytes 12976320 | tf_op jit(solution)/shard_map/ctk,tkn->tcn/dot_general | solution.py:86
  18.2 12.9 %scatter_fusion = f32[32,32,512]{2,1,0:T(8,128)S(1)} fusion(f32[32,32,512]{2,1,0:T(8,128)S(1)} %broadcast.79.clone, s32[96]{0:T(128)S(1)} %bitcast.209, f32[96,32,512]{2,1,0:T(8,128)} %broadcast_select_fusion.1), kind=kCustom, calls=%fused_computation.4 | custom fusion | flops 1572864 | bytes 18874752 | tf_op jit(solution)/shard_map/scatter-add | solution.py:100
  41.8 6.5 %broadcast_select_fusion = f32[96,32,512]{2,1,0:T(8,128)} fusion(pred[96]{0:T(512)(128)(4,1)S(1)} %iota_compare_fusion, bf16[1,96,64,512]{3,2,1,0:T(8,128)(2,1)} %param.21, bf16[96,32,64]{2,1,0:T(8,128)(2,1)S(1)} %gather_fusion.2, pred[96]{0:T(512)(128)(4,1)S(1)} %get-tuple-element.115), kind=kOutput, calls=%fused_computation.46 | convolution fusion | flops 203096064 | bytes 12976320 | tf_op jit(solution)/shard_map/ctk,tkn->tcn/dot_general | solution.py:86
  48.6 12.9 %scatter_fusion.2 = f32[32,32,512]{2,1,0:T(8,128)S(1)} fusion(f32[32,32,512]{2,1,0:T(8,128)S(1)} %broadcast.79.clone.1, s32[96]{0:T(128)S(1)} %bitcast.210, f32[96,32,512]{2,1,0:T(8,128)} %broadcast_select_fusion), kind=kCustom, calls=%fused_computation.6 | custom fusion | flops 1572864 | bytes 18874752 | tf_op jit(solution)/shard_map/scatter-add | solution.py:100
  85.2 4.0 collective-permute-start.9
  115.3 3.9 pad_maximum_fusion.8
  119.2 3.9 reshape.269
  123.1 3.9 pad_maximum_fusion.5
  127.0 3.5 reshape.266
  130.5 3.5 reshape.265
  134.0 3.9 pad_maximum_fusion.4
  138.0 3.5 reshape.264
  147.1 3.5 reshape.267
  150.7 3.9 pad_maximum_fusion.7
  169.3 3.8 fusion.12
  173.2 3.7 fusion.10
  200.7 4.0 pad_maximum_fusion.15
  207.5 3.5 reshape.284
  211.0 4.0 pad_maximum_fusion.14
  218.5 3.9 pad_maximum_fusion.13
  222.4 3.5 reshape.282
  226.0 3.9 pad_maximum_fusion.12
  229.9 3.5 reshape.281
  233.5 3.9 pad_maximum_fusion.11
  257.9 3.9 collective-permute-start.11
  266.3 3.8 collective-permute-start.5
  270.1 76.8 %all-reduce.2.cloned.1.call-done = f32[27,32,32]{1,2,0:T(8,128)} async-done(((f32[27,32,32]{1,2,0:T(8,128)}), f32[27,32,32]{1,2,0:T(8,128)}) %all-reduce.2.cloned.1.call-update) | async-done | bytes 110608 | tf_op jit(solution)/shard_map/psum | solution.py:157
  353.6 5.6 %fusion.52 = f32[96,32,64]{2,1,0:T(8,128)S(1)} fusion(bf16[1,96,64,512]{3,2,1,0:T(8,128)(2,1)} %param.21, bf16[96,32,512]{2,1,0:T(8,128)(2,1)} %gather_fusion.3, pred[96]{0:T(512)(128)(4,1)S(1)} %get-tuple-element.114, pred[96]{0:T(512)(128)(4,1)S(1)} %iota_compare_fusion), kind=kOutput, calls=%fused_computation.92 | convolution fusion | flops 203096064 | bytes 10223808 | tf_op jit(solution)/shard_map/ctn,tkn->tck/dot_general | solution.py:93
  359.3 4.5 scatter_fusion.3
  365.0 63.5 %psum.15 = f32[32,32]{1,0:T(8,128)S(1)} all-reduce(f32[32,32]{1,0:T(8,128)S(1)} %fusion.69), channel_id=1, replica_groups=mesh['rep'=8,'slab'=16] {'rep','slab'}, use_global_device_ids=true, to_apply=%region_5.8 | all-reduce | flops 1024 | bytes 8192 | tf_op jit(solution)/shard_map/psum | solution.py:157
  434.7 5.6 %fusion.47 = f32[96,32,64]{2,1,0:T(8,128)S(1)} fusion(bf16[1,96,64,512]{3,2,1,0:T(8,128)(2,1)} %param.21, bf16[96,32,512]{2,1,0:T(8,128)(2,1)} %gather_fusion.1, pred[96]{0:T(512)(128)(4,1)S(1)} %get-tuple-element.114, pred[96]{0:T(512)(128)(4,1)S(1)} %iota_compare_fusion), kind=kOutput, calls=%fused_computation.91 | convolution fusion | flops 203096064 | bytes 10223808 | tf_op jit(solution)/shard_map/ctn,tkn->tck/dot_general | solution.py:93
  440.3 4.5 scatter_fusion.1
  (224 shorter events, 154.5 us)
Async XLA Ops:
  7.2 2.1 copy-start
  7.2 339.8 %all-reduce.2.cloned.1.call-start = ((), (), s32[]{:S(2)}) async-start(), calls=%async_computation | async-start | bytes 884736 | tf_op jit(solution)/shard_map/psum | solution.py:157
  35.9 5.0 %copy-start.30 = (bf16[1,32,1536]{2,1,0:T(8,128)(2,1)S(1)}, bf16[1,32,1536]{2,1,0:T(8,128)(2,1)}, u32[]{:S(2)}) copy-start(bf16[1,32,1536]{2,1,0:T(8,128)(2,1)} %param.27) | copy-start | bytes 294916
  38.1 39.7 %collective-permute-start = (bf16[32,2,2048]{2,0,1:T(8,128)(2,1)}, bf16[32,2,2048]{2,0,1:T(8,128)(2,1)S(1)}, u32[]{:S(2)}, u32[]{:S(2)}) collective-permute-start(bf16[32,2,2048]{2,0,1:T(8,128)(2,1)} %get-tuple-element.97), channel_id=1, source_target_pairs={{0,1},{1,2},{2,3},{3,4},{4,5},{5,6},{6,7},{7,8},{8,9},{9,10},{10,1... | collective-permute-start | bytes 786440 | tf_op jit(solution)/shard_map/ppermute | solution.py:23
  40.7 38.3 %collective-permute-start.1 = (bf16[32,2,2048]{2,0,1:T(8,128)(2,1)}, bf16[32,2,2048]{2,0,1:T(8,128)(2,1)S(1)}, u32[]{:S(2)}, u32[]{:S(2)}) collective-permute-start(bf16[32,2,2048]{2,0,1:T(8,128)(2,1)} %get-tuple-element.96), channel_id=1, source_target_pairs={{0,15},{1,0},{2,1},{3,2},{4,3},{5,4},{6,5},{7,6},{8,7},{9,8},{10,9... | collective-permute-start | bytes 786440 | tf_op jit(solution)/shard_map/ppermute | solution.py:23
  66.3 4.7 %copy-start.19 = (bf16[27,32,32]{2,1,0:T(8,128)(2,1)S(1)}, bf16[27,32,32]{2,1,0:T(8,128)(2,1)}, u32[]{:S(2)}) copy-start(bf16[27,32,32]{2,1,0:T(8,128)(2,1)} %param.26) | copy-start | bytes 165892
  66.3 4.7 %copy-start.3 = (f32[32,8,2048]{2,1,0:T(8,128)S(1)}, f32[32,8,2048]{2,1,0:T(8,128)}, u32[]{:S(2)}) copy-start(f32[32,8,2048]{2,1,0:T(8,128)} %copy-done.2) | copy-start | bytes 6291460
  68.3 14.9 %collective-permute-start.6 = (bf16[32,2,2048]{2,0,1:T(8,128)(2,1)}, bf16[32,2,2048]{2,0,1:T(8,128)(2,1)}, u32[]{:S(2)}, u32[]{:S(2)}) collective-permute-start(bf16[32,2,2048]{2,0,1:T(8,128)(2,1)} %get-tuple-element.95), channel_id=1, source_target_pairs={{0,1},{1,2},{2,3},{3,4},{4,5},{5,6},{6,7},{7,8},{8,9},{9,10},{10,1... | collective-permute-start | bytes 786440 | tf_op jit(solution)/shard_map/ppermute | solution.py:23
  70.0 14.2 %collective-permute-start.7 = (bf16[32,2,2048]{2,0,1:T(8,128)(2,1)}, bf16[32,2,2048]{2,0,1:T(8,128)(2,1)S(1)}, u32[]{:S(2)}, u32[]{:S(2)}) collective-permute-start(bf16[32,2,2048]{2,0,1:T(8,128)(2,1)} %get-tuple-element.94), channel_id=1, source_target_pairs={{0,15},{1,0},{2,1},{3,2},{4,3},{5,4},{6,5},{7,6},{8,7},{9,8},{10,9... | collective-permute-start | bytes 786440 | tf_op jit(solution)/shard_map/ppermute | solution.py:23
  73.6 4.2 slice-start.3
  79.0 4.3 copy-start.5
  79.0 4.3 slice-start.2
  79.2 9.9 %collective-permute-start.2 = (bf16[32,1,2048]{2,0,1:T(8,128)(2,1)S(1)}, bf16[32,1,2048]{2,0,1:T(8,128)(2,1)S(1)}, u32[]{:S(2)}, u32[]{:S(2)}) collective-permute-start(bf16[32,1,2048]{2,0,1:T(8,128)(2,1)S(1)} %get-tuple-element.104), channel_id=1, source_target_pairs={{0,1},{1,2},{2,3},{3,4},{4,5},{5,6},{6,7},{7,8},{8,9},{9,10},{10,1... | collective-permute-start | bytes 393224 | tf_op jit(solution)/shard_map/ppermute | solution.py:32
  80.1 9.0 %collective-permute-start.3 = (bf16[32,1,2048]{2,0,1:T(8,128)(2,1)S(1)}, bf16[32,1,2048]{2,0,1:T(8,128)(2,1)S(1)}, u32[]{:S(2)}, u32[]{:S(2)}) collective-permute-start(bf16[32,1,2048]{2,0,1:T(8,128)(2,1)S(1)} %get-tuple-element.105), channel_id=1, source_target_pairs={{1,0},{2,1},{3,2},{4,3},{5,4},{6,5},{7,6},{8,7},{9,8},{10,9},{11,1... | collective-permute-start | bytes 393224 | tf_op jit(solution)/shard_map/ppermute | solution.py:35
  85.2 93.1 %collective-permute-start.8 = (bf16[32,1,2048]{2,0,1:T(8,128)(2,1)}, bf16[32,1,2048]{2,0,1:T(8,128)(2,1)}, u32[]{:S(2)}, u32[]{:S(2)}) collective-permute-start(bf16[32,1,2048]{2,0,1:T(8,128)(2,1)} %get-tuple-element.100), channel_id=1, source_target_pairs={{0,1},{1,2},{2,3},{3,4},{4,5},{5,6},{6,7},{7,8},{8,9},{9,10},{10,1... | collective-permute-start | bytes 393224 | tf_op jit(solution)/shard_map/ppermute | solution.py:32
  85.2 93.1 %collective-permute-start.9 = (bf16[32,1,2048]{2,0,1:T(8,128)(2,1)}, bf16[32,1,2048]{2,0,1:T(8,128)(2,1)}, u32[]{:S(2)}, u32[]{:S(2)}) collective-permute-start(bf16[32,1,2048]{2,0,1:T(8,128)(2,1)} %get-tuple-element.101), channel_id=1, source_target_pairs={{1,0},{2,1},{3,2},{4,3},{5,4},{6,5},{7,6},{8,7},{9,8},{10,9},{11,1... | collective-permute-start | bytes 393224 | tf_op jit(solution)/shard_map/ppermute | solution.py:35
  141.5 2.2 copy-start.7
  160.3 2.3 copy-start.12
  160.3 3.2 copy-start.16
  162.6 1.9 copy-start.21
  162.6 1.9 copy-start.23
  165.5 1.9 copy-start.14
  169.3 7.6 %copy-start.1 = (bf16[288,6,2048]{2,0,1:T(8,128)(2,1)S(1)}, bf16[288,6,2048]{2,0,1:T(8,128)(2,1)}, u32[]{:S(2)}) copy-start(bf16[288,6,2048]{2,0,1:T(8,128)(2,1)} %constant_dynamic-update-slice_fusion) | copy-start | bytes 21233668
  255.3 6.6 %slice-start = ((s8[7077888]{0:T(1024)(128)(4,1)}), s8[4194304]{0:T(1024)(128)(4,1)S(1)}, s32[]{:S(2)}) async-start(s8[7077888]{0:T(1024)(128)(4,1)} %bitcast.196), calls=%async_computation.1 | async-start | bytes 8388608
  256.5 5.3 %slice-start.1 = ((s8[7077888]{0:T(1024)(128)(4,1)}), s8[2883584]{0:T(1024)(128)(4,1)S(1)}, s32[]{:S(2)}) async-start(s8[7077888]{0:T(1024)(128)(4,1)} %bitcast.196), calls=%async_computation.2 | async-start | bytes 5767168
  256.5 5.3 %copy-start.25 = (bf16[32,9,32]{0,2,1:T(8,128)(2,1)S(1)}, bf16[32,9,32]{0,2,1:T(8,128)(2,1)}, u32[]{:S(2)}) copy-start(bf16[32,9,32]{0,2,1:T(8,128)(2,1)} %copy.50) | copy-start | bytes 55300
  257.8 91.1 %collective-permute-start.10 = (bf16[32,2,2048]{2,0,1:T(8,128)(2,1)S(1)}, bf16[32,2,2048]{2,0,1:T(8,128)(2,1)S(1)}, u32[]{:S(2)}, u32[]{:S(2)}) collective-permute-start(bf16[32,2,2048]{2,0,1:T(8,128)(2,1)S(1)} %get-tuple-element.98), channel_id=1, source_target_pairs={{0,1},{1,2},{2,3},{3,4},{4,5},{5,6},{6,7},{7,8},{8,9},{9,10},{10,1... | collective-permute-start | bytes 786440 | tf_op jit(solution)/shard_map/ppermute | solution.py:32
  257.9 91.0 %collective-permute-start.11 = (bf16[32,2,2048]{2,0,1:T(8,128)(2,1)S(1)}, bf16[32,2,2048]{2,0,1:T(8,128)(2,1)S(1)}, u32[]{:S(2)}, u32[]{:S(2)}) collective-permute-start(bf16[32,2,2048]{2,0,1:T(8,128)(2,1)S(1)} %get-tuple-element.99), channel_id=1, source_target_pairs={{1,0},{2,1},{3,2},{4,3},{5,4},{6,5},{7,6},{8,7},{9,8},{10,9},{11,1... | collective-permute-start | bytes 786440 | tf_op jit(solution)/shard_map/ppermute | solution.py:35
  266.3 162.9 %collective-permute-start.4 = (bf16[32,2,2048]{2,0,1:T(8,128)(2,1)}, bf16[32,2,2048]{2,0,1:T(8,128)(2,1)}, u32[]{:S(2)}, u32[]{:S(2)}) collective-permute-start(bf16[32,2,2048]{2,0,1:T(8,128)(2,1)} %get-tuple-element.102), channel_id=1, source_target_pairs={{0,1},{1,2},{2,3},{3,4},{4,5},{5,6},{6,7},{7,8},{8,9},{9,10},{10,1... | collective-permute-start | bytes 786440 | tf_op jit(solution)/shard_map/ppermute | solution.py:32
  266.3 162.9 %collective-permute-start.5 = (bf16[32,2,2048]{2,0,1:T(8,128)(2,1)S(1)}, bf16[32,2,2048]{2,0,1:T(8,128)(2,1)}, u32[]{:S(2)}, u32[]{:S(2)}) collective-permute-start(bf16[32,2,2048]{2,0,1:T(8,128)(2,1)S(1)} %get-tuple-element.103), channel_id=1, source_target_pairs={{1,0},{2,1},{3,2},{4,3},{5,4},{6,5},{7,6},{8,7},{9,8},{10,9},{11,1... | collective-permute-start | bytes 786440 | tf_op jit(solution)/shard_map/ppermute | solution.py:35
  353.6 5.6 %copy-start.33 = (s32[1,96]{1,0:T(1,128)S(1)}, s32[1,96]{1,0:T(1,128)}, u32[]{:S(2)}) copy-start(s32[1,96]{1,0:T(1,128)} %param.22) | copy-start | bytes 1156
  359.2 4.9 %copy-start.31 = (bf16[32,32]{1,0:T(8,128)(2,1)S(1)}, bf16[32,32]{1,0:T(8,128)(2,1)}, u32[]{:S(2)}) copy-start(bf16[32,32]{1,0:T(8,128)(2,1)} %param.25) | copy-start | bytes 6148
  (19 other events, 23.7 us)
Sparse Core Ops, SparseCore 0:
  200.8 146.0 all-reduce.1
where the time goes:
time: 460 us; the launch traced here: 453 us
  local copies, waits for them, and re-layouts  118 us (26%)
  other arithmetic  115 us (25%)
  waiting for transfers between devices  76.9 us (17%)
  blocking collectives  63.5 us (14%)
  matrix products  42.3 us (9%)
  starting transfers between devices  21.2 us (5%)
  between operations  15.8 us (3%)
    psum x1, waiting for transfers between devices, local(): conv_total, mix_total = lax.psum((conv_part, mix_part), ('rep', 'slab'))  76.8 us
    concatenate x24, other arithmetic, shifted_stack(): rolled = jnp.roll(shaped, (-row_off, -col_off), (2, 3))  69.1 us
    psum x1, blocking collectives, local(): conv_total, mix_total = lax.psum((conv_part, mix_part), ('rep', 'slab'))  63.5 us
    reshape x16, local copies, waits for them, and re-layouts, shifted_stack(): pieces.append(rolled.reshape(C, planes, GY * GX))  51.4 us
    scatter-add x4, other arithmetic, over_tiles(): return jax.ops.segment_sum(products, target_ids, num_segments=segments)  34.8 us
    unnamed x87, local copies, waits for them, and re-layouts  18.3 us
    ppermute x4, starting transfers between devices, extended_2(): lax.ppermute(lax.slice_in_dim(block, 0, width, axis=dim), axis, backward)  14.8 us
    dot_general x2, matrix products, deposit_tiles(): jnp.einsum('ctk,tkn->tcn', picked, weights, preferred_element_type=jnp.fl...  13 us
  transfers between devices with their start and end apart: 13, of which 1 were waited for; matrix products, arithmetic and copies ran while one was open for 44% of the time, Pallas kernels for 0%

commit v1 on v0

--- a/solution.py
+++ b/solution.py
@@ -154,7 +154,7 @@
     mix_part = lax.dot_general(
         mixed_grad, atom_feats, (((1,), (1,)), ((), ())), preferred_element_type=jnp.float32
     )
-    conv_total, mix_total = lax.psum((conv_part, mix_part), ("rep", "slab"))
+    conv_total, mix_total = lax.psum(lax.psum((conv_part, mix_part), "rep"), "slab")
     groups = lax.axis_size("rep") * lax.axis_size("slab")
     conv_scale = math.sqrt(groups * ZD * GY * GX)
     mix_scale = math.sqrt(groups * A_DEV)

time: 460 us -> 550 us (1.20)
  waiting for transfers between devices: 76.9 us -> 135 us
  blocking collectives: 63.5 us -> 91.4 us
    psum x1 -> x2, waiting for transfers between devices: 76.8 us -> 134 us  [the longest x1 114 us: local(): lax.psum(lax.psum((conv_part, mix_part), 'rep'), 'slab')]
    psum x1 -> x2, blocking collectives: 63.5 us -> 91.4 us  [the longest x1 56.3 us: local(): lax.psum(lax.psum((conv_part, mix_part), 'rep'), 'slab')]
  transfers between devices with their start and end apart: 13 -> 14, of which waited for: 1 -> 2; matrix products, arithmetic and copies ran while one was open for 44% -> 37% of each run, Pallas kernels for 0% -> 0%
where the time goes in v1:
time: 550 us; the launch traced here: 540 us
  waiting for transfers between devices  135 us (25%)
  local copies, waits for them, and re-layouts  119 us (22%)
  other arithmetic  115 us (21%)
  blocking collectives  91.4 us (17%)
  matrix products  42.3 us (8%)
  starting transfers between devices  22.9 us (4%)
  between operations  15.8 us (3%)
    psum x1, waiting for transfers between devices, local(): lax.psum(lax.psum((conv_part, mix_part), 'rep'), 'slab')  114 us
    concatenate x24, other arithmetic, shifted_stack(): rolled = jnp.roll(shaped, (-row_off, -col_off), (2, 3))  69 us
    psum x1, blocking collectives, local(): lax.psum(lax.psum((conv_part, mix_part), 'rep'), 'slab')  56.3 us
    reshape x16, local copies, waits for them, and re-layouts, shifted_stack(): pieces.append(rolled.reshape(C, planes, GY * GX))  51.5 us
    psum x1, blocking collectives, local(): lax.psum((conv_part, mix_part), 'rep')  35.1 us
    scatter-add x4, other arithmetic, over_tiles(): return jax.ops.segment_sum(products, target_ids, num_segments=segments)  34.8 us
    psum x1, waiting for transfers between devices, local(): lax.psum((conv_part, mix_part), 'rep')  20.7 us
    unnamed x87, local copies, waits for them, and re-layouts  18.4 us
  transfers between devices with their start and end apart: 14, of which 2 were waited for; matrix products, arithmetic and copies ran while one was open for 37% of the time, Pallas kernels for 0%

profile of v1, /device:TPU:1, one launch (start us, length us, event | category | flops | bytes accessed | tf_op | source)
XLA Modules:
  0.0 540.1 jit_solution(8881976732160677149)
XLA Ops:
  11.0 6.5 %broadcast_select_fusion.1 = f32[96,32,512]{2,1,0:T(8,128)} fusion(pred[96]{0:T(512)(128)(4,1)S(1)} %iota_compare_fusion, bf16[1,96,64,512]{3,2,1,0:T(8,128)(2,1)} %param.21, bf16[96,32,64]{2,1,0:T(8,128)(2,1)S(1)} %gather_fusion, pred[96]{0:T(512)(128)(4,1)S(1)} %get-tuple-element.115), kind=kOutput, calls=%fused_computation.47 | convolution fusion | flops 203096064 | bytes 12976320 | tf_op jit(solution)/shard_map/ctk,tkn->tcn/dot_general | solution.py:86
  18.2 12.9 %scatter_fusion = f32[32,32,512]{2,1,0:T(8,128)S(1)} fusion(f32[32,32,512]{2,1,0:T(8,128)S(1)} %broadcast.79.clone, s32[96]{0:T(128)S(1)} %bitcast.209, f32[96,32,512]{2,1,0:T(8,128)} %broadcast_select_fusion.1), kind=kCustom, calls=%fused_computation.4 | custom fusion | flops 1572864 | bytes 18874752 | tf_op jit(solution)/shard_map/scatter-add | solution.py:100
  41.9 6.5 %broadcast_select_fusion = f32[96,32,512]{2,1,0:T(8,128)} fusion(pred[96]{0:T(512)(128)(4,1)S(1)} %iota_compare_fusion, bf16[1,96,64,512]{3,2,1,0:T(8,128)(2,1)} %param.21, bf16[96,32,64]{2,1,0:T(8,128)(2,1)S(1)} %gather_fusion.2, pred[96]{0:T(512)(128)(4,1)S(1)} %get-tuple-element.115), kind=kOutput, calls=%fused_computation.46 | convolution fusion | flops 203096064 | bytes 12976320 | tf_op jit(solution)/shard_map/ctk,tkn->tcn/dot_general | solution.py:86
  48.7 12.9 %scatter_fusion.2 = f32[32,32,512]{2,1,0:T(8,128)S(1)} fusion(f32[32,32,512]{2,1,0:T(8,128)S(1)} %broadcast.79.clone.1, s32[96]{0:T(128)S(1)} %bitcast.210, f32[96,32,512]{2,1,0:T(8,128)} %broadcast_select_fusion), kind=kCustom, calls=%fused_computation.6 | custom fusion | flops 1572864 | bytes 18874752 | tf_op jit(solution)/shard_map/scatter-add | solution.py:100
  85.3 4.0 collective-permute-start.9
  115.4 3.9 pad_maximum_fusion.8
  119.3 3.9 reshape.269
  123.2 3.9 pad_maximum_fusion.5
  127.1 3.5 reshape.266
  134.2 3.9 pad_maximum_fusion.4
  138.1 3.6 reshape.264
  147.3 3.6 reshape.267
  150.9 3.9 pad_maximum_fusion.7
  169.5 3.8 fusion.12
  173.4 3.7 fusion.10
  201.0 4.0 pad_maximum_fusion.15
  207.8 3.5 reshape.284
  211.3 3.9 pad_maximum_fusion.14
  218.8 3.9 pad_maximum_fusion.13
  226.3 3.9 pad_maximum_fusion.12
  230.2 3.6 reshape.281
  233.8 3.9 pad_maximum_fusion.11
  258.2 3.9 collective-permute-start.11
  265.9 20.7 %all-reduce.3.cloned.1.call-done = f32[27,32,32]{1,2,0:T(8,128)} async-done(((f32[27,32,32]{1,2,0:T(8,128)}), f32[27,32,32]{1,2,0:T(8,128)}) %all-reduce.3.cloned.1.call-update) | async-done | bytes 110608 | tf_op jit(solution)/shard_map/psum | solution.py:157
  287.3 5.4 collective-permute-start.4
  292.7 113.8 %all-reduce.5.cloned.1.call-done = f32[27,32,32]{1,2,0:T(8,128)} async-done(((f32[27,32,32]{1,2,0:T(8,128)}), f32[27,32,32]{1,2,0:T(8,128)}) %all-reduce.5.cloned.1.call-update) | async-done | bytes 110608 | tf_op jit(solution)/shard_map/psum | solution.py:157
  413.1 5.6 %fusion.52 = f32[96,32,64]{2,1,0:T(8,128)S(1)} fusion(bf16[1,96,64,512]{3,2,1,0:T(8,128)(2,1)} %param.21, bf16[96,32,512]{2,1,0:T(8,128)(2,1)} %gather_fusion.3, pred[96]{0:T(512)(128)(4,1)S(1)} %get-tuple-element.114, pred[96]{0:T(512)(128)(4,1)S(1)} %iota_compare_fusion), kind=kOutput, calls=%fused_computation.92 | convolution fusion | flops 203096064 | bytes 10223808 | tf_op jit(solution)/shard_map/ctn,tkn->tck/dot_general | solution.py:93
  418.8 4.5 scatter_fusion.3
  424.6 35.1 %psum.30 = f32[32,32]{1,0:T(8,128)S(1)} all-reduce(f32[32,32]{1,0:T(8,128)S(1)} %fusion.69), channel_id=1, replica_groups=mesh['rep'=8,'slab'=16] {'rep'}, use_global_device_ids=true, to_apply=%region_6.9 | all-reduce | flops 1024 | bytes 8192 | tf_op jit(solution)/shard_map/psum | solution.py:157
  459.7 56.3 %psum.31 = f32[32,32]{1,0:T(8,128)S(1)} all-reduce(f32[32,32]{1,0:T(8,128)S(1)} %psum.30), channel_id=1, replica_groups=mesh['rep'=8,'slab'=16] {'slab'}, use_global_device_ids=true, to_apply=%region_7.10 | all-reduce | flops 1024 | bytes 8192 | tf_op jit(solution)/shard_map/psum | solution.py:157
  522.1 5.6 %fusion.47 = f32[96,32,64]{2,1,0:T(8,128)S(1)} fusion(bf16[1,96,64,512]{3,2,1,0:T(8,128)(2,1)} %param.21, bf16[96,32,512]{2,1,0:T(8,128)(2,1)} %gather_fusion.1, pred[96]{0:T(512)(128)(4,1)S(1)} %get-tuple-element.114, pred[96]{0:T(512)(128)(4,1)S(1)} %iota_compare_fusion), kind=kOutput, calls=%fused_computation.91 | convolution fusion | flops 203096064 | bytes 10223808 | tf_op jit(solution)/shard_map/ctn,tkn->tck/dot_general | solution.py:93
  527.7 4.5 scatter_fusion.1
  (228 shorter events, 161.7 us)
Async XLA Ops:
  7.2 2.1 copy-start
  7.2 279.4 %all-reduce.3.cloned.1.call-start = ((), (), s32[]{:S(2)}) async-start(), calls=%async_computation | async-start | bytes 884736 | tf_op jit(solution)/shard_map/psum | solution.py:157
  36.0 5.0 copy-start.30
  38.2 39.8 %collective-permute-start = (bf16[32,2,2048]{2,0,1:T(8,128)(2,1)}, bf16[32,2,2048]{2,0,1:T(8,128)(2,1)S(1)}, u32[]{:S(2)}, u32[]{:S(2)}) collective-permute-start(bf16[32,2,2048]{2,0,1:T(8,128)(2,1)} %get-tuple-element.97), channel_id=1, source_target_pairs={{0,1},{1,2},{2,3},{3,4},{4,5},{5,6},{6,7},{7,8},{8,9},{9,10},{10,1... | collective-permute-start | bytes 786440 | tf_op jit(solution)/shard_map/ppermute | solution.py:23
  40.8 38.3 %collective-permute-start.1 = (bf16[32,2,2048]{2,0,1:T(8,128)(2,1)}, bf16[32,2,2048]{2,0,1:T(8,128)(2,1)S(1)}, u32[]{:S(2)}, u32[]{:S(2)}) collective-permute-start(bf16[32,2,2048]{2,0,1:T(8,128)(2,1)} %get-tuple-element.96), channel_id=1, source_target_pairs={{0,15},{1,0},{2,1},{3,2},{4,3},{5,4},{6,5},{7,6},{8,7},{9,8},{10,9... | collective-permute-start | bytes 786440 | tf_op jit(solution)/shard_map/ppermute | solution.py:23
  66.4 4.7 copy-start.19
  66.4 4.7 copy-start.3
  68.4 15.0 %collective-permute-start.6 = (bf16[32,2,2048]{2,0,1:T(8,128)(2,1)}, bf16[32,2,2048]{2,0,1:T(8,128)(2,1)}, u32[]{:S(2)}, u32[]{:S(2)}) collective-permute-start(bf16[32,2,2048]{2,0,1:T(8,128)(2,1)} %get-tuple-element.95), channel_id=1, source_target_pairs={{0,1},{1,2},{2,3},{3,4},{4,5},{5,6},{6,7},{7,8},{8,9},{9,10},{10,1... | collective-permute-start | bytes 786440 | tf_op jit(solution)/shard_map/ppermute | solution.py:23
  70.1 14.2 %collective-permute-start.7 = (bf16[32,2,2048]{2,0,1:T(8,128)(2,1)}, bf16[32,2,2048]{2,0,1:T(8,128)(2,1)S(1)}, u32[]{:S(2)}, u32[]{:S(2)}) collective-permute-start(bf16[32,2,2048]{2,0,1:T(8,128)(2,1)} %get-tuple-element.94), channel_id=1, source_target_pairs={{0,15},{1,0},{2,1},{3,2},{4,3},{5,4},{6,5},{7,6},{8,7},{9,8},{10,9... | collective-permute-start | bytes 786440 | tf_op jit(solution)/shard_map/ppermute | solution.py:23
  73.7 4.3 slice-start.3
  79.1 4.3 copy-start.5
  79.1 4.3 slice-start.2
  79.3 9.9 %collective-permute-start.2 = (bf16[32,1,2048]{2,0,1:T(8,128)(2,1)S(1)}, bf16[32,1,2048]{2,0,1:T(8,128)(2,1)S(1)}, u32[]{:S(2)}, u32[]{:S(2)}) collective-permute-start(bf16[32,1,2048]{2,0,1:T(8,128)(2,1)S(1)} %get-tuple-element.104), channel_id=1, source_target_pairs={{0,1},{1,2},{2,3},{3,4},{4,5},{5,6},{6,7},{7,8},{8,9},{9,10},{10,1... | collective-permute-start | bytes 393224 | tf_op jit(solution)/shard_map/ppermute | solution.py:32
  80.2 9.1 %collective-permute-start.3 = (bf16[32,1,2048]{2,0,1:T(8,128)(2,1)S(1)}, bf16[32,1,2048]{2,0,1:T(8,128)(2,1)S(1)}, u32[]{:S(2)}, u32[]{:S(2)}) collective-permute-start(bf16[32,1,2048]{2,0,1:T(8,128)(2,1)S(1)} %get-tuple-element.105), channel_id=1, source_target_pairs={{1,0},{2,1},{3,2},{4,3},{5,4},{6,5},{7,6},{8,7},{9,8},{10,9},{11,1... | collective-permute-start | bytes 393224 | tf_op jit(solution)/shard_map/ppermute | solution.py:35
  85.3 93.2 %collective-permute-start.8 = (bf16[32,1,2048]{2,0,1:T(8,128)(2,1)}, bf16[32,1,2048]{2,0,1:T(8,128)(2,1)}, u32[]{:S(2)}, u32[]{:S(2)}) collective-permute-start(bf16[32,1,2048]{2,0,1:T(8,128)(2,1)} %get-tuple-element.100), channel_id=1, source_target_pairs={{0,1},{1,2},{2,3},{3,4},{4,5},{5,6},{6,7},{7,8},{8,9},{9,10},{10,1... | collective-permute-start | bytes 393224 | tf_op jit(solution)/shard_map/ppermute | solution.py:32
  85.3 93.2 %collective-permute-start.9 = (bf16[32,1,2048]{2,0,1:T(8,128)(2,1)}, bf16[32,1,2048]{2,0,1:T(8,128)(2,1)}, u32[]{:S(2)}, u32[]{:S(2)}) collective-permute-start(bf16[32,1,2048]{2,0,1:T(8,128)(2,1)} %get-tuple-element.101), channel_id=1, source_target_pairs={{1,0},{2,1},{3,2},{4,3},{5,4},{6,5},{7,6},{8,7},{9,8},{10,9},{11,1... | collective-permute-start | bytes 393224 | tf_op jit(solution)/shard_map/ppermute | solution.py:35
  141.6 2.2 copy-start.7
  160.5 2.3 copy-start.12
  160.5 3.3 copy-start.16
  162.8 2.0 copy-start.21
  162.8 2.0 copy-start.23
  169.5 7.6 %copy-start.1 = (bf16[288,6,2048]{2,0,1:T(8,128)(2,1)S(1)}, bf16[288,6,2048]{2,0,1:T(8,128)(2,1)}, u32[]{:S(2)}) copy-start(bf16[288,6,2048]{2,0,1:T(8,128)(2,1)} %constant_dynamic-update-slice_fusion) | copy-start | bytes 21233668
  201.0 205.5 %all-reduce.5.cloned.1.call-start = ((), (), s32[]{:S(2)}) async-start(), calls=%async_computation.1 | async-start | bytes 884736 | tf_op jit(solution)/shard_map/psum | solution.py:157
  255.5 6.6 %slice-start = ((s8[7077888]{0:T(1024)(128)(4,1)}), s8[4194304]{0:T(1024)(128)(4,1)S(1)}, s32[]{:S(2)}) async-start(s8[7077888]{0:T(1024)(128)(4,1)} %bitcast.196), calls=%async_computation.2 | async-start | bytes 8388608
  256.8 5.3 slice-start.1
  256.8 5.3 copy-start.25
  258.1 150.4 %collective-permute-start.10 = (bf16[32,2,2048]{2,0,1:T(8,128)(2,1)S(1)}, bf16[32,2,2048]{2,0,1:T(8,128)(2,1)S(1)}, u32[]{:S(2)}, u32[]{:S(2)}) collective-permute-start(bf16[32,2,2048]{2,0,1:T(8,128)(2,1)S(1)} %get-tuple-element.98), channel_id=1, source_target_pairs={{0,1},{1,2},{2,3},{3,4},{4,5},{5,6},{6,7},{7,8},{8,9},{9,10},{10,1... | collective-permute-start | bytes 786440 | tf_op jit(solution)/shard_map/ppermute | solution.py:32
  258.2 150.3 %collective-permute-start.11 = (bf16[32,2,2048]{2,0,1:T(8,128)(2,1)S(1)}, bf16[32,2,2048]{2,0,1:T(8,128)(2,1)S(1)}, u32[]{:S(2)}, u32[]{:S(2)}) collective-permute-start(bf16[32,2,2048]{2,0,1:T(8,128)(2,1)S(1)} %get-tuple-element.99), channel_id=1, source_target_pairs={{1,0},{2,1},{3,2},{4,3},{5,4},{6,5},{7,6},{8,7},{9,8},{10,9},{11,1... | collective-permute-start | bytes 786440 | tf_op jit(solution)/shard_map/ppermute | solution.py:35
  287.3 229.2 %collective-permute-start.4 = (bf16[32,2,2048]{2,0,1:T(8,128)(2,1)}, bf16[32,2,2048]{2,0,1:T(8,128)(2,1)}, u32[]{:S(2)}, u32[]{:S(2)}) collective-permute-start(bf16[32,2,2048]{2,0,1:T(8,128)(2,1)} %get-tuple-element.102), channel_id=1, source_target_pairs={{0,1},{1,2},{2,3},{3,4},{4,5},{5,6},{6,7},{7,8},{8,9},{9,10},{10,1... | collective-permute-start | bytes 786440 | tf_op jit(solution)/shard_map/ppermute | solution.py:32
  292.7 223.9 %collective-permute-start.5 = (bf16[32,2,2048]{2,0,1:T(8,128)(2,1)S(1)}, bf16[32,2,2048]{2,0,1:T(8,128)(2,1)}, u32[]{:S(2)}, u32[]{:S(2)}) collective-permute-start(bf16[32,2,2048]{2,0,1:T(8,128)(2,1)S(1)} %get-tuple-element.103), channel_id=1, source_target_pairs={{1,0},{2,1},{3,2},{4,3},{5,4},{6,5},{7,6},{8,7},{9,8},{10,9},{11,1... | collective-permute-start | bytes 786440 | tf_op jit(solution)/shard_map/ppermute | solution.py:35
  413.1 5.6 %copy-start.33 = (s32[1,96]{1,0:T(1,128)S(1)}, s32[1,96]{1,0:T(1,128)}, u32[]{:S(2)}) copy-start(s32[1,96]{1,0:T(1,128)} %param.22) | copy-start | bytes 1156
  418.8 4.9 copy-start.31
  (20 other events, 25.7 us)
Sparse Core Ops, SparseCore 0:
  201.1 85.4 all-reduce.2
  289.2 117.2 all-reduce.4
